TPU v7x, 32 devices: a whole 2x2x4 slice. The times are simulated.
32 devices in a mesh: groups: 2 (over y), row: 8 (over z, x), col: 2 (over core).
Axes of the slice: x: 2, y: 2, z: 4, core: 2. Of those that a mesh axis runs over, the one named last changes fastest.
Arguments:
- queries: float32 [128, 4096], P(('groups', 'row'), 'col'), parts along dimension 0, may hold values from -3 to 3
- documents: float32 [128, 4096], P(('groups', 'row'), 'col'), parts along dimension 0, may hold values from -3 to 3
- positive: int32 [128], P(('groups', 'row')), parts along dimension 0, may hold values from 0 to 63, as said below
- hard_ids: int32 [128, 7], P(('groups', 'row')), parts along dimension 0, may hold values from 0 to 63
Outputs:
- request_derivative: float32 [128, 4096], P(('groups', 'row'), 'col'), parts along dimension 0
- passage_derivative: float32 [128, 4096], P(('groups', 'row'), 'col'), parts along dimension 0
- loss_rows: float32 [128], P(('groups', 'row')), parts along dimension 0
There are 2 independent parts, one for each index of `groups`. A program takes and returns all parts, laid end to end along the dimension named above; each array names one. Nothing has to cross between parts.
Inputs may be any that keep to these rules, and one draw needn't show every extreme that they name: positive[i] is a document of query i's own aligned block of 8, from i - i % 8 to i - i % 8 + 7; within each block every document is the positive of exactly one query.
All inputs are finite; a program needn't handle non-finite values.
Results may differ from a plain program's by a relative error of at most 0.006.
Values may be sent and summed in bfloat16 or wider, within the bound.
A program may use at most 64 MiB of HBM per device.

v0:
```python
import jax
import jax.numpy as jnp
from jax import lax
from jax.sharding import PartitionSpec as P

sharpness_divisor = 0.05
hardness_multiplier = 3.0


def weigh(request_similarity, passage_similarity, positive, hard_ids, batch_size):
    columns = jnp.arange(batch_size, dtype=jnp.int32)
    hardness_tally = jnp.zeros(request_similarity.shape, jnp.float32)
    for column in range(hard_ids.shape[1]):
        hardness_tally = hardness_tally + (hard_ids[:, column][:, None] == columns[None, :]).astype(
            jnp.float32
        )
    request_raw_similarity = request_similarity / sharpness_divisor + jnp.log1p(
        hardness_multiplier * hardness_tally
    )
    matching_indicator = positive[:, None] == columns[None, :]
    passage_raw_similarity = jnp.where(
        matching_indicator, -jnp.inf, passage_similarity / sharpness_divisor
    )
    row_peak = jnp.maximum(
        jnp.max(request_raw_similarity, axis=1), jnp.max(passage_raw_similarity, axis=1)
    )
    row_mass = jnp.sum(jnp.exp(request_raw_similarity - row_peak[:, None]), axis=1) + jnp.sum(
        jnp.exp(passage_raw_similarity - row_peak[:, None]), axis=1
    )
    row_lse = row_peak + jnp.log(row_mass)
    loss_rows = row_lse - jnp.sum(
        jnp.where(matching_indicator, request_raw_similarity, 0.0), axis=1
    )
    request_probability = jnp.exp(request_raw_similarity - row_lse[:, None]).astype(jnp.bfloat16)
    passage_probability = jnp.exp(passage_raw_similarity - row_lse[:, None]).astype(jnp.bfloat16)
    return (request_probability, passage_probability, loss_rows)


def contract_first(left, right):
    return lax.dot_general(
        left, right, (((0,), (0,)), ((), ())), preferred_element_type=jnp.float32
    )


def on_device(queries, documents, positive, hard_ids):
    row_count = queries.shape[0]
    batch_size = row_count * lax.axis_size("row")
    offset = lax.axis_index("row") * row_count
    request_matrix = queries.astype(jnp.bfloat16)
    passage_matrix = documents.astype(jnp.bfloat16)
    local_pos = positive - offset
    picker = local_pos[:, None] == jnp.arange(row_count, dtype=jnp.int32)[None, :]
    reference_side_entries = jnp.take(passage_matrix, local_pos, axis=0)
    document_gathered, query_all = (
        lax.all_gather(passage_matrix, "row", axis=0, tiled=True),
        lax.all_gather(request_matrix, "row", axis=0, tiled=True),
    )
    stacked = jnp.concatenate([request_matrix, reference_side_entries], axis=0)
    partial_value = lax.dot_general(
        stacked, document_gathered, (((1,), (1,)), ((), ())), preferred_element_type=jnp.float32
    )
    query_part = partial_value[:row_count]
    doc_part = partial_value[row_count:]
    request_similarity, passage_similarity = lax.psum((query_part, doc_part), "col")
    request_probability, passage_probability, loss_rows = weigh(
        request_similarity, passage_similarity, positive, hard_ids, batch_size
    )
    request_derivative = (
        jnp.dot(request_probability, document_gathered, preferred_element_type=jnp.float32)
        - reference_side_entries.astype(jnp.float32)
    ) / sharpness_divisor
    reference_side_derivative = (
        jnp.dot(passage_probability, document_gathered, preferred_element_type=jnp.float32)
        / sharpness_divisor
    )
    forwarded_entries = (
        reference_side_derivative - request_matrix.astype(jnp.float32) / sharpness_divisor
    )
    permuted = contract_first(picker.astype(jnp.bfloat16), passage_probability).astype(jnp.bfloat16)
    query_columns, anchor_columns = (
        lax.all_to_all(request_probability, "row", split_axis=1, concat_axis=0, tiled=True),
        lax.all_to_all(permuted, "row", split_axis=1, concat_axis=0, tiled=True),
    )
    anchor_contribution = contract_first(anchor_columns, document_gathered)
    query_contribution = contract_first(query_columns, query_all)
    dispersion_level = lax.dot_general(
        picker.astype(jnp.float32),
        forwarded_entries,
        (((0,), (0,)), ((), ())),
        precision=lax.Precision.HIGHEST,
        preferred_element_type=jnp.float32,
    )
    passage_derivative = (
        query_contribution + anchor_contribution
    ) / sharpness_divisor + dispersion_level
    return (request_derivative, passage_derivative, loss_rows)


def solution(mesh):
    return jax.shard_map(
        on_device,
        mesh=mesh,
        in_specs=(
            P(("groups", "row"), "col"),
            P(("groups", "row"), "col"),
            P(("groups", "row")),
            P(("groups", "row"), None),
        ),
        out_specs=(P(("groups", "row"), "col"), P(("groups", "row"), "col"), P(("groups", "row"))),
        check_vma=False,
    )
```

profile of v0, /device:TPU:0, one launch (start us, length us, event | category | flops | bytes accessed | tf_op | source)
XLA Modules:
  0.0 89.3 jit_solution(14401006248320287965)
XLA Ops:
  0.6 0.6 copy-done.2
  1.3 0.8 convert_element_type.45
  2.2 32.5 %all_gather.6 = bf16[64,2048]{1,0:T(8,128)(2,1)S(1)} all-gather(bf16[8,2048]{1,0:T(8,128)(2,1)S(1)} %convert_element_type.45), channel_id=1, replica_groups=mesh['groups'=2,'row'=8,'col'=2] {'row'}, dimensions={0}, use_global_device_ids=true | all-gather | bytes 294912 | tf_op jit(solution)/shard_map/all_gather | solution.py:55
  34.7 0.6 gather_fusion
  35.3 0.3 copy-done.1
  35.6 0.2 fusion.3
  35.8 0.7 copy-done
  36.5 0.3 slice_reduce_fusion.6
  36.7 2.5 %all-reduce = (f32[8,64]{1,0:T(8,128)S(1)}, f32[8,64]{1,0:T(8,128)S(1)}) all-reduce(f32[8,64]{1,0:T(8,128)S(1)} %get-tuple-element.22, f32[8,64]{1,0:T(8,128)S(1)} %get-tuple-element.21), channel_id=1, replica_groups=mesh['groups'=2,'row'=8,'col'=2] {'col'}, use_global_device_ids=true, to_apply=%region_0.1 | all-reduce | flops 1024 | bytes 8192 | tf_op jit(solution)/shard_map/psum | solution.py:64
  39.2 0.2 fusion.12
  39.4 0.2 select_reduce_fusion
  39.7 0.5 fusion.11
  40.3 0.7 copy.13
  41.0 5.5 %all-to-all-start = ((bf16[8,8,8]{0,2,1:T(8,128)(2,1)}), bf16[8,8,8]{0,2,1:T(8,128)(2,1)S(1)}, u32[]{:S(2)}, u32[]{:S(2)}) async-start(bf16[8,8,8]{0,2,1:T(8,128)(2,1)} %bitcast), calls=%async_computation | async-start | bytes 32768 | tf_op jit(solution)/shard_map/all_to_all | solution.py:81
  46.5 0.8 fusion.2
  47.3 0.2 fusion
  47.4 0.3 convolution_convert_fusion
  47.7 0.7 copy.14
  48.4 4.7 %all-to-all-done = bf16[8,8,8]{0,2,1:T(8,128)(2,1)S(1)} async-done(((bf16[8,8,8]{0,2,1:T(8,128)(2,1)}), bf16[8,8,8]{0,2,1:T(8,128)(2,1)S(1)}, u32[]{:S(2)}, u32[]{:S(2)}) %all-to-all-start) | async-done | bytes 1056 | tf_op jit(solution)/shard_map/all_to_all | solution.py:81
  53.1 3.3 %all-to-all-start.1 = ((bf16[8,8,8]{0,2,1:T(8,128)(2,1)}), bf16[8,8,8]{0,2,1:T(8,128)(2,1)S(1)}, u32[]{:S(2)}, u32[]{:S(2)}) async-start(bf16[8,8,8]{0,2,1:T(8,128)(2,1)} %bitcast.2), calls=%async_computation.1 | async-start | bytes 32768 | tf_op jit(solution)/shard_map/all_to_all | solution.py:82
  56.4 31.4 %all_gather.7 = bf16[64,2048]{1,0:T(8,128)(2,1)S(1)} all-gather(bf16[8,2048]{1,0:T(8,128)(2,1)S(1)} %convert_element_type.44), channel_id=1, replica_groups=mesh['groups'=2,'row'=8,'col'=2] {'row'}, dimensions={0}, use_global_device_ids=true | all-gather | bytes 294912 | tf_op jit(solution)/shard_map/all_gather | solution.py:56
  88.0 0.1 fusion.14
  88.2 0.2 fusion.1
  88.4 0.9 %convolution_add_fusion = f32[8,2048]{1,0:T(8,128)} fusion(f32[8,2048]{1,0:T(8,128)S(1)} %fusion.1, f32[8,2048]{1,0:T(8,128)S(1)} %fusion, s32[8]{0:T(128)S(1)} %get-tuple-element.20), kind=kOutput, calls=%fused_computation.1 | convolution fusion | flops 1589312 | bytes 196640 | tf_op jit(solution)/shard_map/dot_general | solution.py:86
  (16 shorter events, 0.4 us)
Async XLA Ops:
  0.6 0.7 copy-start.2
  34.7 0.8 copy-start.1
  35.8 0.7 copy-start
  41.0 12.1 %all-to-all-start = ((bf16[8,8,8]{0,2,1:T(8,128)(2,1)}), bf16[8,8,8]{0,2,1:T(8,128)(2,1)S(1)}, u32[]{:S(2)}, u32[]{:S(2)}) async-start(bf16[8,8,8]{0,2,1:T(8,128)(2,1)} %bitcast), calls=%async_computation | async-start | bytes 32768 | tf_op jit(solution)/shard_map/all_to_all | solution.py:81
  53.1 34.9 %all-to-all-start.1 = ((bf16[8,8,8]{0,2,1:T(8,128)(2,1)}), bf16[8,8,8]{0,2,1:T(8,128)(2,1)S(1)}, u32[]{:S(2)}, u32[]{:S(2)}) async-start(bf16[8,8,8]{0,2,1:T(8,128)(2,1)} %bitcast.2), calls=%async_computation.1 | async-start | bytes 32768 | tf_op jit(solution)/shard_map/all_to_all | solution.py:82
where the time goes:
time: 89.7 us; the launch traced here: 89.3 us
  blocking collectives  66.4 us (74%)
  starting transfers between devices  8.86 us (10%)
  waiting for transfers between devices  4.7 us (5%)
  local copies, waits for them, and re-layouts  4.02 us (4%)
  matrix products  2.58 us (3%)
  other arithmetic  1.98 us (2%)
    all_gather x1, blocking collectives, on_device(): lax.all_gather(passage_matrix, 'row', axis=0, tiled=True)  32.5 us
    all_gather x1, blocking collectives, on_device(): lax.all_gather(request_matrix, 'row', axis=0, tiled=True)  31.4 us
    all_to_all x1, starting transfers between devices, on_device(): lax.all_to_all(request_probability, 'row', split_axis=1, concat_axis=0, t...  5.52 us
    all_to_all x1, waiting for transfers between devices, on_device(): lax.all_to_all(request_probability, 'row', split_axis=1, concat_axis=0, t...  4.7 us
    all_to_all x1, starting transfers between devices, on_device(): lax.all_to_all(permuted, 'row', split_axis=1, concat_axis=0, tiled=True)  3.33 us
    psum x1, blocking collectives, on_device(): lax.psum((query_part, doc_part), 'col')  2.5 us
  transfers between devices with their start and end apart: 2, of which 1 were waited for; matrix products, arithmetic and copies ran while one was open for 2% of the time, Pallas kernels for 0%

commit v1 on v0

v1 whole, which is shorter than its diff:
```python
import functools

import jax
import jax.numpy as jnp
from jax import lax
from jax.experimental import pallas as pl
from jax.experimental.pallas import tpu as pltpu
from jax.sharding import PartitionSpec as P

inverse_temperature = 20.0
hardness_multiplier = 3.0
MESH = pl.DeviceIdType.MESH
LANES = 128


def repeat(count, body):
    if count <= 8:
        for step in range(count):
            body(step)
    else:
        lax.fori_loop(0, count, lambda step, carry: (body(step), carry)[1], 0)


def kernel(
    n,
    q_hbm,
    d_hbm,
    pos_hbm,
    hid_hbm,
    req_ref,
    pas_ref,
    loss_ref,
    q_in,
    d_in,
    pos_in,
    hid_in,
    table,
    scores,
    landed,
    flipped,
    in_sem,
    send_sem,
    recv_sem,
    col_sem,
):
    rows, width = q_in.shape
    pair_rows = 2 * rows
    total = pair_rows * n
    chunks = total // LANES
    per_chunk = LANES // pair_rows
    me = lax.axis_index("row")
    core = lax.axis_index("col")
    depth = n // 2
    z, x = me // 2, me % 2
    twin = z * 2 + (1 - x)

    def line_peer(step):
        return lax.rem(z + step + 1, depth) * 2 + x

    def line_source(step):
        return lax.rem(z + depth - step - 1, depth) * 2 + x

    loads = [
        pltpu.make_async_copy(src, dst, in_sem.at[i])
        for i, (src, dst) in enumerate(
            ((pos_hbm, pos_in), (q_hbm, q_in), (d_hbm, d_in), (hid_hbm, hid_in))
        )
    ]
    for load in loads:
        load.start()

    barrier = pltpu.get_barrier_semaphore()

    def greet(step):
        pl.semaphore_signal(
            barrier, inc=1, device_id={"row": line_peer(step)}, device_id_type=MESH
        )

    repeat(depth - 1, greet)
    pl.semaphore_signal(barrier, inc=1, device_id={"row": twin}, device_id_type=MESH)
    pl.semaphore_signal(barrier, inc=1, device_id={"col": 1 - core}, device_id_type=MESH)

    for load in loads:
        load.wait()

    places = [pos_in[i] - me * rows for i in range(rows)]

    def to_documents(value):
        at = lax.broadcasted_iota(jnp.int32, value.shape, 0)
        out = jnp.zeros_like(value)
        for i in range(rows):
            out = jnp.where(at == places[i], value[i : i + 1, :], out)
        return out

    def to_queries(value):
        at = lax.broadcasted_iota(jnp.int32, value.shape, 0)
        place = jnp.zeros(value.shape, jnp.int32)
        for i in range(rows):
            place = jnp.where(at == i, places[i], place)
        out = jnp.zeros_like(value)
        for t in range(rows):
            out = jnp.where(place == t, value[t : t + 1, :], out)
        return out

    mine = pl.ds(pl.multiple_of(me * pair_rows, pair_rows), pair_rows)
    queries = to_documents(q_in[...])
    documents = d_in[...]
    lane = lax.broadcasted_iota(jnp.int32, (rows, total), 1)
    within = lax.rem(lane, pair_rows)
    document_id = jnp.where(
        within >= rows, lane // pair_rows * rows + within - rows, -1
    )
    hard = hid_in[...]
    tally = jnp.zeros((rows, total), jnp.float32)
    for k in range(hard.shape[1]):
        tally = tally + jnp.where(hard[:, k : k + 1] == document_id, 1.0, 0.0)
    table[mine, :width] = jnp.concatenate([queries, documents], axis=0).astype(jnp.bfloat16)
    table[mine, width:] = jnp.concatenate(
        [to_documents(tally), jnp.zeros_like(tally)], axis=0
    ).astype(jnp.bfloat16)

    pl.semaphore_wait(barrier, depth + 1)

    def block_copy(source, target, slot):
        block = table.at[pl.ds(pl.multiple_of(source * pair_rows, pair_rows), pair_rows)]
        return pltpu.make_async_remote_copy(
            src_ref=block,
            dst_ref=block,
            send_sem=send_sem.at[slot],
            recv_sem=recv_sem.at[source],
            device_id={"row": target},
            device_id_type=MESH,
        )

    block_copy(me, twin, 0).start()
    repeat(depth - 1, lambda step: block_copy(me, line_peer(step), 1 + step).start())

    def forward(step):
        source = line_source(step)
        block_copy(source, twin, depth + step).wait_recv()
        block_copy(source, twin, depth + step).start()

    repeat(depth - 1, forward)
    block_copy(twin, twin, 0).wait_recv()
    repeat(
        depth - 1,
        lambda step: block_copy(line_source(step) + 1 - 2 * x, twin, 0).wait_recv(),
    )

    def part(c):
        start = c * LANES
        return pl.ds(start if isinstance(c, int) else pl.multiple_of(start, LANES), LANES)

    def multiply(c):
        def against(e):
            scores[part(c), part(e)] = lax.dot_general(
                table[part(c), :width],
                table[part(e), :width],
                (((1,), (1,)), ((), ())),
                preferred_element_type=jnp.float32,
            )

        repeat(chunks, against)

    repeat(chunks, multiply)

    exchange = pltpu.make_async_remote_copy(
        src_ref=scores,
        dst_ref=landed,
        send_sem=col_sem.at[0],
        recv_sem=col_sem.at[1],
        device_id={"col": 1 - core},
        device_id_type=MESH,
    )
    exchange.start()

    half = (per_chunk, rows, total)
    column = lax.broadcasted_iota(jnp.int32, half, 2)
    is_document = lax.rem(column, pair_rows) >= rows
    own_column = (
        lax.broadcasted_iota(jnp.int32, half, 0) * pair_rows
        + lax.broadcasted_iota(jnp.int32, half, 1)
        + rows
    )

    def bias_of(c):
        counts = table[part(c), width:].astype(jnp.float32)
        counts = counts.reshape(per_chunk, pair_rows, total)[:, :rows]
        return jnp.log(1.0 + hardness_multiplier * counts)

    early = bias_of(0) if chunks == 1 else None
    exchange.wait()

    def weigh(c):
        bias = early if chunks == 1 else bias_of(c)
        logits = (scores[part(c), :] + landed[part(c), :]) * inverse_temperature
        logits = logits.reshape(per_chunk, pair_rows, total)
        is_positive = column == own_column + c * LANES
        query_logits = jnp.where(is_document, logits[:, :rows] + bias, -jnp.inf)
        doc_logits = jnp.where(
            is_document & jnp.logical_not(is_positive), logits[:, rows:], -jnp.inf
        )
        peak = jnp.max(jnp.maximum(query_logits, doc_logits), axis=2, keepdims=True)
        mass = jnp.sum(
            jnp.exp(query_logits - peak) + jnp.exp(doc_logits - peak), axis=2, keepdims=True
        )
        lse = peak + jnp.log(mass)
        losses = lse - jnp.sum(jnp.where(is_positive, query_logits, 0.0), axis=2, keepdims=True)
        weights = jnp.concatenate(
            [jnp.exp(query_logits - lse), jnp.exp(doc_logits - lse)], axis=1
        )
        scores[part(c), :] = weights.reshape(LANES, total)
        landed[part(c), :LANES] = jnp.broadcast_to(
            jnp.concatenate([losses, losses], axis=1), (per_chunk, pair_rows, LANES)
        ).reshape(LANES, LANES)

    repeat(chunks, weigh)

    upper = pl.ds(pl.multiple_of(me * pair_rows, rows), rows)
    lower = pl.ds(pl.multiple_of(me * pair_rows + rows, rows), rows)
    query_part = to_queries(scores[upper, :])
    doc_part = scores[lower, :]
    own_tile = pl.ds(pl.multiple_of(me // per_chunk * LANES, LANES), LANES)
    own_rows = pl.ds(
        pl.multiple_of(lax.rem(me, per_chunk) * pair_rows + rows, rows), rows
    )

    losses = landed[upper, :LANES]
    at = lax.broadcasted_iota(jnp.int32, losses.shape, 0)
    across = lax.broadcasted_iota(jnp.int32, losses.shape, 1)
    place = jnp.full(losses.shape, -1, jnp.int32)
    for i in range(rows):
        place = jnp.where(across == i, places[i], place)
    loss_ref[...] = jnp.sum(jnp.where(place == at, losses, 0.0), axis=0, keepdims=True)[:, :rows]

    if chunks > 1:
        landed[: 2 * rows, :total] = jnp.concatenate([query_part, doc_part], axis=0)
        req_ref[...] = jnp.zeros_like(req_ref)
        pas_ref[...] = jnp.zeros_like(pas_ref)

    def derive(c):
        flipped[...] = scores[part(c), own_tile].T
        if chunks > 1:
            heads = landed[: 2 * rows, part(c)]
        else:
            heads = jnp.concatenate([query_part, doc_part], axis=0)
        left = jnp.concatenate([heads, flipped[own_rows, :]], axis=0)
        out = jnp.dot(
            left.astype(jnp.bfloat16), table[part(c), :width], preferred_element_type=jnp.float32
        )
        request, passage = out[:rows], out[rows : 2 * rows] + out[2 * rows :]
        if chunks > 1:
            request, passage = req_ref[...] + request, pas_ref[...] + passage
        if chunks == 1 or isinstance(c, int):
            pass
        req_ref[...] = request
        pas_ref[...] = passage

    repeat(chunks, derive)
    own = table[mine, :width].astype(jnp.float32)
    req_ref[...] = (req_ref[...] - to_queries(own[rows:])) * inverse_temperature
    pas_ref[...] = (pas_ref[...] - own[:rows]) * inverse_temperature

    block_copy(me, twin, 0).wait_send()
    repeat(depth - 1, lambda step: block_copy(me, twin, 1 + step).wait_send())
    repeat(depth - 1, lambda step: block_copy(me, twin, depth + step).wait_send())


def on_device(queries, documents, positive, hard_ids):
    n = lax.axis_size("row")
    rows, width = queries.shape
    total = 2 * rows * n
    vmem = pl.BlockSpec(memory_space=pltpu.VMEM)
    request, passage, losses = pl.pallas_call(
        functools.partial(kernel, n),
        out_shape=(
            jax.ShapeDtypeStruct((rows, width), jnp.float32),
            jax.ShapeDtypeStruct((rows, width), jnp.float32),
            jax.ShapeDtypeStruct((1, rows), jnp.float32),
        ),
        in_specs=[pl.BlockSpec(memory_space=pl.ANY)] * 4,
        out_specs=(vmem, vmem, vmem),
        scratch_shapes=[
            pltpu.VMEM((rows, width), jnp.float32),
            pltpu.VMEM((rows, width), jnp.float32),
            pltpu.SMEM((rows,), jnp.int32),
            pltpu.VMEM(hard_ids.shape, jnp.int32),
            pltpu.VMEM((total, width + total), jnp.bfloat16),
            pltpu.VMEM((total, total), jnp.float32),
            pltpu.VMEM((total, total), jnp.float32),
            pltpu.VMEM((LANES, LANES), jnp.float32),
            pltpu.SemaphoreType.DMA((4,)),
            pltpu.SemaphoreType.DMA((n - 1,)),
            pltpu.SemaphoreType.DMA((n,)),
            pltpu.SemaphoreType.DMA((2,)),
        ],
        compiler_params=pltpu.CompilerParams(
            collective_id=0, has_side_effects=True, vmem_limit_bytes=60 * 1024 * 1024
        ),
    )(queries, documents, positive, hard_ids)
    return request, passage, losses.reshape(rows)


def solution(mesh):
    return jax.shard_map(
        on_device,
        mesh=mesh,
        in_specs=(
            P(("groups", "row"), "col"),
            P(("groups", "row"), "col"),
            P(("groups", "row")),
            P(("groups", "row"), None),
        ),
        out_specs=(P(("groups", "row"), "col"), P(("groups", "row"), "col"), P(("groups", "row"))),
        check_vma=False,
    )
```

time: 89.7 us -> 22 us (0.25)
  blocking collectives: 66.4 us -> 0 us
  Pallas kernels: 0 us -> 18.5 us
  starting transfers between devices: 8.86 us -> 0 us
  waiting for transfers between devices: 4.7 us -> 0 us
  matrix products: 2.58 us -> 0 us
  other arithmetic: 1.98 us -> 0 us
  local copies, waits for them, and re-layouts: 4.02 us -> 2.65 us
    all_gather x2 -> x0, blocking collectives: 63.9 us -> none  [the longest x1 32.5 us: on_device(): lax.all_gather(passage_matrix, 'row', axis=0, tiled=True)]
    pallas_call x0 -> x1, Pallas kernels: none -> 18.5 us  [on_device(): pl.pallas_call(functools.partial(kernel, n), out_shape=(jax.ShapeDtypeStr...]
    all_to_all x2 -> x0, starting transfers between devices: 8.86 us -> none  [the longest x1 5.52 us: on_device(): lax.all_to_all(request_probability, 'row', split_axis=1, concat_axis=0, t...]
    all_to_all x2 -> x0, waiting for transfers between devices: 4.7 us -> none  [the longest x1 4.7 us: on_device(): lax.all_to_all(request_probability, 'row', split_axis=1, concat_axis=0, t...]
    dot_general x7 -> x0, matrix products: 2.58 us -> none  [the longest x1 0.92 us: on_device(): lax.dot_general(picker.astype(jnp.float32), forwarded_entries, (((0,), (0...]
    psum x1 -> x0, blocking collectives: 2.5 us -> none  [on_device(): lax.psum((query_part, doc_part), 'col')]
    all_to_all x6 -> x0, local copies, waits for them, and re-layouts: 1.58 us -> none  [the longest x3 0.8 us: on_device(): lax.all_to_all(request_probability, 'row', split_axis=1, concat_axis=0, t...]
    unnamed x6 -> x7, local copies, waits for them, and re-layouts: 1.61 us -> 2.65 us
  transfers between devices with their start and end apart: 2 -> 0, of which waited for: 1 -> 0; matrix products, arithmetic and copies ran while one was open for 2% -> 0% of each run, Pallas kernels for 0% -> 0%
where the time goes in v1:
time: 22 us; the launch traced here: 21.8 us
  Pallas kernels  18.5 us (84%)
  local copies, waits for them, and re-layouts  2.65 us (12%)
  between operations  0.65 us (3%)
    pallas_call x1, Pallas kernels, on_device(): pl.pallas_call(functools.partial(kernel, n), out_shape=(jax.ShapeDtypeStr...  18.5 us
    unnamed x7, local copies, waits for them, and re-layouts  2.65 us

profile of v1, /device:TPU:0, one launch (start us, length us, event | category | flops | bytes accessed | tf_op | source)
XLA Modules:
  0.0 21.8 jit_solution(10509083969714745543)
XLA Ops:
  0.6 18.5 %shard_map.67 = (f32[8,2048]{1,0:T(8,128)}, f32[8,2048]{1,0:T(8,128)}, f32[1,8]{1,0:T(1,128)}) custom-call(f32[8,2048]{1,0:T(8,128)} %q_hbm.1, f32[8,2048]{1,0:T(8,128)} %d_hbm.1, s32[8]{0:T(128)} %pos_hbm.1, s32[8,7]{1,0:T(8,128)} %hid_hbm.1), custom_call_target="tpu_custom_call" | custom-call | tf_op jit(solution)/shard_map/pallas_call | solution.py:274
  19.2 0.0 copy-start
  19.2 1.5 %copy.10 = f32[8,2048]{1,0:T(8,128)} copy(f32[8,2048]{1,0:T(8,128)} %get-tuple-element.12) | data formatting | bytes 131072
  20.7 0.0 copy-done
  20.7 0.0 copy-start.1
  20.7 0.6 %copy.11 = f32[8,2048]{1,0:T(8,128)} copy(f32[8,2048]{1,0:T(8,128)S(1)} %copy-done) | data formatting | bytes 131072
  21.3 0.0 copy-done.1
  21.3 0.5 %copy.12 = f32[8]{0:T(128)} copy(f32[8]{0:T(128)S(1)} %bitcast.1) | data formatting | bytes 64
Async XLA Ops:
  19.2 1.5 %copy-start = (f32[8,2048]{1,0:T(8,128)S(1)}, f32[8,2048]{1,0:T(8,128)}, u32[]{:S(2)}) copy-start(f32[8,2048]{1,0:T(8,128)} %get-tuple-element.13) | copy-start | bytes 196612
  20.7 0.6 %copy-start.1 = (f32[1,8]{1,0:T(1,128)S(1)}, f32[1,8]{1,0:T(1,128)}, u32[]{:S(2)}) copy-start(f32[1,8]{1,0:T(1,128)} %get-tuple-element.8) | copy-start | bytes 100

commit v2 on v1

--- a/solution.py
+++ b/solution.py
@@ -11,6 +11,7 @@
 hardness_multiplier = 3.0
 MESH = pl.DeviceIdType.MESH
 LANES = 128
+PIECES = 2
 
 
 def repeat(count, body):
@@ -27,14 +28,13 @@
     d_hbm,
     pos_hbm,
     hid_hbm,
-    req_ref,
-    pas_ref,
+    table,
+    left_ref,
     loss_ref,
     q_in,
     d_in,
     pos_in,
     hid_in,
-    table,
     scores,
     landed,
     flipped,
@@ -106,9 +106,9 @@
     queries = to_documents(q_in[...])
     documents = d_in[...]
     lane = lax.broadcasted_iota(jnp.int32, (rows, total), 1)
-    within = lax.rem(lane, pair_rows)
+    within = lane & (pair_rows - 1)
     document_id = jnp.where(
-        within >= rows, lane // pair_rows * rows + within - rows, -1
+        within >= rows, (lane - within) // 2 + within - rows, -1
     )
     hard = hid_in[...]
     tally = jnp.zeros((rows, total), jnp.float32)
@@ -176,7 +176,7 @@
 
     half = (per_chunk, rows, total)
     column = lax.broadcasted_iota(jnp.int32, half, 2)
-    is_document = lax.rem(column, pair_rows) >= rows
+    is_document = (column & rows) != 0
     own_column = (
         lax.broadcasted_iota(jnp.int32, half, 0) * pair_rows
         + lax.broadcasted_iota(jnp.int32, half, 1)
@@ -187,6 +187,19 @@
         counts = table[part(c), width:].astype(jnp.float32)
         counts = counts.reshape(per_chunk, pair_rows, total)[:, :rows]
         return jnp.log(1.0 + hardness_multiplier * counts)
+
+    tile = (rows, LANES)
+    tile_row = lax.broadcasted_iota(jnp.int32, tile, 0)
+    tile_lane = lax.broadcasted_iota(jnp.int32, tile, 1)
+    across_place = jnp.full(tile, -1, jnp.int32)
+    down_place = jnp.zeros(tile, jnp.int32)
+    for i in range(rows):
+        across_place = jnp.where(tile_lane == i, places[i], across_place)
+        down_place = jnp.where(tile_row == i, places[i], down_place)
+
+    def anchor_rows(c):
+        at = tile_lane + c * LANES - (me * pair_rows + rows)
+        return jnp.where(at == down_place, -1.0, 0.0)
 
     early = bias_of(0) if chunks == 1 else None
     exchange.wait()
@@ -218,52 +231,59 @@
 
     upper = pl.ds(pl.multiple_of(me * pair_rows, rows), rows)
     lower = pl.ds(pl.multiple_of(me * pair_rows + rows, rows), rows)
-    query_part = to_queries(scores[upper, :])
-    doc_part = scores[lower, :]
+    sublane = lax.broadcasted_iota(jnp.int32, (rows, total), 0)
+    heads = jnp.where(lane == me * pair_rows + sublane, -1.0, scores[lower, :])
+    left_ref[: 2 * rows, :] = jnp.concatenate(
+        [to_queries(scores[upper, :]), heads], axis=0
+    ).astype(jnp.bfloat16)
     own_tile = pl.ds(pl.multiple_of(me // per_chunk * LANES, LANES), LANES)
     own_rows = pl.ds(
         pl.multiple_of(lax.rem(me, per_chunk) * pair_rows + rows, rows), rows
     )
 
+    def columns(c):
+        flipped[...] = scores[part(c), own_tile].T
+        left_ref[2 * rows :, part(c)] = jnp.concatenate(
+            [flipped[own_rows, :], anchor_rows(c)], axis=0
+        ).astype(jnp.bfloat16)
+
+    repeat(chunks, columns)
+
     losses = landed[upper, :LANES]
     at = lax.broadcasted_iota(jnp.int32, losses.shape, 0)
-    across = lax.broadcasted_iota(jnp.int32, losses.shape, 1)
-    place = jnp.full(losses.shape, -1, jnp.int32)
-    for i in range(rows):
-        place = jnp.where(across == i, places[i], place)
-    loss_ref[...] = jnp.sum(jnp.where(place == at, losses, 0.0), axis=0, keepdims=True)[:, :rows]
-
-    if chunks > 1:
-        landed[: 2 * rows, :total] = jnp.concatenate([query_part, doc_part], axis=0)
-        req_ref[...] = jnp.zeros_like(req_ref)
-        pas_ref[...] = jnp.zeros_like(pas_ref)
-
-    def derive(c):
-        flipped[...] = scores[part(c), own_tile].T
-        if chunks > 1:
-            heads = landed[: 2 * rows, part(c)]
-        else:
-            heads = jnp.concatenate([query_part, doc_part], axis=0)
-        left = jnp.concatenate([heads, flipped[own_rows, :]], axis=0)
-        out = jnp.dot(
-            left.astype(jnp.bfloat16), table[part(c), :width], preferred_element_type=jnp.float32
-        )
-        request, passage = out[:rows], out[rows : 2 * rows] + out[2 * rows :]
-        if chunks > 1:
-            request, passage = req_ref[...] + request, pas_ref[...] + passage
-        if chunks == 1 or isinstance(c, int):
-            pass
-        req_ref[...] = request
-        pas_ref[...] = passage
-
-    repeat(chunks, derive)
-    own = table[mine, :width].astype(jnp.float32)
-    req_ref[...] = (req_ref[...] - to_queries(own[rows:])) * inverse_temperature
-    pas_ref[...] = (pas_ref[...] - own[:rows]) * inverse_temperature
+    loss_ref[...] = jnp.sum(jnp.where(across_place == at, losses, 0.0), axis=0, keepdims=True)
 
     block_copy(me, twin, 0).wait_send()
     repeat(depth - 1, lambda step: block_copy(me, twin, 1 + step).wait_send())
     repeat(depth - 1, lambda step: block_copy(me, twin, depth + step).wait_send())
+
+
+def finish(width, left_ref, table_ref, loss_in, req_hbm, pas_hbm, loss_ref, req, pas, sem):
+    rows = req.shape[0]
+    loss_ref[...] = loss_in[0, :rows]
+    total = left_ref.shape[1]
+    step = width // PIECES
+    copies = []
+    for piece in range(PIECES):
+        across = pl.ds(piece * step, step)
+        out = jnp.zeros((4 * rows, step), jnp.float32)
+        for start in range(0, total, LANES):
+            depth = min(total, LANES)
+            out = out + jnp.dot(
+                left_ref[:, start : start + depth],
+                table_ref[start : start + depth, across],
+                preferred_element_type=jnp.float32,
+            )
+        req[:, across] = (out[:rows] + out[3 * rows :]) * inverse_temperature
+        pas[:, across] = (out[rows : 2 * rows] + out[2 * rows : 3 * rows]) * inverse_temperature
+        for which, (src, dst) in enumerate(((req, req_hbm), (pas, pas_hbm))):
+            copy = pltpu.make_async_copy(
+                src.at[:, across], dst.at[:, across], sem.at[2 * piece + which]
+            )
+            copy.start()
+            copies.append(copy)
+    for copy in copies:
+        copy.wait()
 
 
 def on_device(queries, documents, positive, hard_ids):
@@ -271,21 +291,22 @@
     rows, width = queries.shape
     total = 2 * rows * n
     vmem = pl.BlockSpec(memory_space=pltpu.VMEM)
-    request, passage, losses = pl.pallas_call(
+    anywhere = pl.BlockSpec(memory_space=pl.ANY)
+    inputs = (queries, documents, positive, hard_ids)
+    table, left, losses = pl.pallas_call(
         functools.partial(kernel, n),
         out_shape=(
-            jax.ShapeDtypeStruct((rows, width), jnp.float32),
-            jax.ShapeDtypeStruct((rows, width), jnp.float32),
-            jax.ShapeDtypeStruct((1, rows), jnp.float32),
+            pltpu.VMEM((total, width + total), jnp.bfloat16),
+            pltpu.VMEM((4 * rows, total), jnp.bfloat16),
+            pltpu.VMEM((1, LANES), jnp.float32),
         ),
-        in_specs=[pl.BlockSpec(memory_space=pl.ANY)] * 4,
+        in_specs=[anywhere] * 4,
         out_specs=(vmem, vmem, vmem),
         scratch_shapes=[
             pltpu.VMEM((rows, width), jnp.float32),
             pltpu.VMEM((rows, width), jnp.float32),
             pltpu.SMEM((rows,), jnp.int32),
             pltpu.VMEM(hard_ids.shape, jnp.int32),
-            pltpu.VMEM((total, width + total), jnp.bfloat16),
             pltpu.VMEM((total, total), jnp.float32),
             pltpu.VMEM((total, total), jnp.float32),
             pltpu.VMEM((LANES, LANES), jnp.float32),
@@ -295,10 +316,30 @@
             pltpu.SemaphoreType.DMA((2,)),
         ],
         compiler_params=pltpu.CompilerParams(
-            collective_id=0, has_side_effects=True, vmem_limit_bytes=60 * 1024 * 1024
+            collective_id=0,
+            has_side_effects=True,
+            vmem_limit_bytes=8 * total * total + 6 * 1024 * 1024,
         ),
-    )(queries, documents, positive, hard_ids)
-    return request, passage, losses.reshape(rows)
+    )(*(pltpu.with_memory_space_constraint(a, pltpu.HBM) for a in inputs))
+    table, left, losses = (
+        pltpu.with_memory_space_constraint(a, pltpu.VMEM) for a in (table, left, losses)
+    )
+    return pl.pallas_call(
+        functools.partial(finish, width),
+        out_shape=(
+            jax.ShapeDtypeStruct((rows, width), jnp.float32),
+            jax.ShapeDtypeStruct((rows, width), jnp.float32),
+            jax.ShapeDtypeStruct((rows,), jnp.float32),
+        ),
+        in_specs=[vmem] * 3,
+        out_specs=(anywhere, anywhere, vmem),
+        scratch_shapes=[
+            pltpu.VMEM((rows, width), jnp.float32),
+            pltpu.VMEM((rows, width), jnp.float32),
+            pltpu.SemaphoreType.DMA((2 * PIECES,)),
+        ],
+        compiler_params=pltpu.CompilerParams(vmem_limit_bytes=6 * 1024 * 1024),
+    )(left, table, losses)
 
 
 def solution(mesh):

time: 22 us -> 19.8 us (0.900)
  local copies, waits for them, and re-layouts: 2.65 us -> 0 us
  Pallas kernels: 18.5 us -> 19 us
    unnamed x7 -> x0, local copies, waits for them, and re-layouts: 2.65 us -> none
    pallas_call x1 -> x2, Pallas kernels: 18.5 us -> 19 us  [the longest x1 17.6 us: on_device(): pl.pallas_call(functools.partial(kernel, n), out_shape=(pltpu.VMEM((total...]
where the time goes in v2:
time: 19.8 us; the launch traced here: 19.6 us
  Pallas kernels  19 us (96%)
  between operations  0.64 us (3%)
    pallas_call x1, Pallas kernels, on_device(): pl.pallas_call(functools.partial(kernel, n), out_shape=(pltpu.VMEM((total...  17.6 us
    pallas_call x1, Pallas kernels, on_device(): pl.pallas_call(functools.partial(finish, width), out_shape=(jax.ShapeDtyp...  1.38 us

profile of v2, /device:TPU:0, one launch (start us, length us, event | category | flops | bytes accessed | tf_op | source)
XLA Modules:
  0.0 19.6 jit_solution(8160673422760000460)
XLA Ops:
  0.6 17.6 %shard_map.67 = (bf16[128,2176]{1,0:T(8,128)(2,1)S(1)}, bf16[32,128]{1,0:T(8,128)(2,1)S(1)}, f32[1,128]{1,0:T(1,128)S(1)}) custom-call(f32[8,2048]{1,0:T(8,128)} %q_hbm.1, f32[8,2048]{1,0:T(8,128)} %d_hbm.1, s32[8]{0:T(128)} %pos_hbm.1, s32[8,7]{1,0:T(8,128)} %hid_hbm.1), custom_call_target="tpu_custom_call" | custom-call | tf_op jit(solution)/shard_map/pallas_call | solution.py:296
  18.2 1.4 %shard_map.68 = (f32[8,2048]{1,0:T(8,128)}, f32[8,2048]{1,0:T(8,128)}, f32[8]{0:T(128)}) custom-call(bf16[32,128]{1,0:T(8,128)(2,1)S(1)} %get-tuple-element.6.left_ref, bf16[128,2176]{1,0:T(8,128)(2,1)S(1)} %get-tuple-element.7.table_ref, f32[1,128]{1,0:T(1,128)S(1)} %get-tuple-element.8.loss_in), custom_call_target="tpu_custom_call" | custom-call | tf_op jit(solution)/shard_map/pallas_call | solution.py:327

commit v3 on v2

--- a/solution.py
+++ b/solution.py
@@ -39,7 +39,9 @@
     landed,
     flipped,
     in_sem,
-    send_sem,
+    up_sem,
+    down_sem,
+    side_sem,
     recv_sem,
     col_sem,
 ):
@@ -53,12 +55,10 @@
     depth = n // 2
     z, x = me // 2, me % 2
     twin = z * 2 + (1 - x)
-
-    def line_peer(step):
-        return lax.rem(z + step + 1, depth) * 2 + x
-
-    def line_source(step):
-        return lax.rem(z + depth - step - 1, depth) * 2 + x
+    above, below = z + 1 < depth, z > 0
+
+    def line(place):
+        return place * 2 + x
 
     loads = [
         pltpu.make_async_copy(src, dst, in_sem.at[i])
@@ -71,14 +71,13 @@
 
     barrier = pltpu.get_barrier_semaphore()
 
-    def greet(step):
-        pl.semaphore_signal(
-            barrier, inc=1, device_id={"row": line_peer(step)}, device_id_type=MESH
-        )
-
-    repeat(depth - 1, greet)
-    pl.semaphore_signal(barrier, inc=1, device_id={"row": twin}, device_id_type=MESH)
-    pl.semaphore_signal(barrier, inc=1, device_id={"col": 1 - core}, device_id_type=MESH)
+    def greet(device):
+        pl.semaphore_signal(barrier, inc=1, device_id=device, device_id_type=MESH)
+
+    greet({"row": twin})
+    greet({"col": 1 - core})
+    pl.when(above)(lambda: greet({"row": line(z + 1)}))
+    pl.when(below)(lambda: greet({"row": line(z - 1)}))
 
     for load in loads:
         load.wait()
@@ -119,50 +118,81 @@
         [to_documents(tally), jnp.zeros_like(tally)], axis=0
     ).astype(jnp.bfloat16)
 
-    pl.semaphore_wait(barrier, depth + 1)
-
-    def block_copy(source, target, slot):
-        block = table.at[pl.ds(pl.multiple_of(source * pair_rows, pair_rows), pair_rows)]
+    pl.semaphore_wait(barrier, 2 + above.astype(jnp.int32) + below.astype(jnp.int32))
+
+    halves = (pl.ds(0, width // 2), pl.ds(width // 2, width // 2 + total))
+
+    def block_copy(source, half, target, sem):
+        block = table.at[
+            pl.ds(pl.multiple_of(source * pair_rows, pair_rows), pair_rows), halves[half]
+        ]
         return pltpu.make_async_remote_copy(
             src_ref=block,
             dst_ref=block,
-            send_sem=send_sem.at[slot],
-            recv_sem=recv_sem.at[source],
+            send_sem=sem,
+            recv_sem=recv_sem.at[source, half],
             device_id={"row": target},
             device_id_type=MESH,
         )
 
-    block_copy(me, twin, 0).start()
-    repeat(depth - 1, lambda step: block_copy(me, line_peer(step), 1 + step).start())
-
-    def forward(step):
-        source = line_source(step)
-        block_copy(source, twin, depth + step).wait_recv()
-        block_copy(source, twin, depth + step).start()
-
-    repeat(depth - 1, forward)
-    block_copy(twin, twin, 0).wait_recv()
-    repeat(
-        depth - 1,
-        lambda step: block_copy(line_source(step) + 1 - 2 * x, twin, 0).wait_recv(),
-    )
+    def upward(place, half):
+        return block_copy(line(place), half, line(z + 1), up_sem.at[place, half])
+
+    def downward(place, half):
+        return block_copy(line(place), half, line(z - 1), down_sem.at[place, half])
+
+    def sideward(place, half):
+        return block_copy(line(place), half, twin, side_sem.at[place, half])
+
+    def arrival(source, half):
+        block_copy(source, half, twin, side_sem.at[0, half]).wait_recv()
+
+    for half in range(2):
+        pl.when(above)(lambda: upward(z, half).start())
+        pl.when(below)(lambda: downward(z, half).start())
+        sideward(z, half).start()
+
+    def relay(step):
+        low, high = z - step - 1, z + step + 1
+        for half in range(2):
+
+            @pl.when(low >= 0)
+            def _():
+                arrival(line(low), half)
+                pl.when(above)(lambda: upward(low, half).start())
+                sideward(low, half).start()
+
+            @pl.when(high < depth)
+            def _():
+                arrival(line(high), half)
+                pl.when(below)(lambda: downward(high, half).start())
+                sideward(high, half).start()
+
+    repeat(depth - 1, relay)
 
     def part(c):
         start = c * LANES
         return pl.ds(start if isinstance(c, int) else pl.multiple_of(start, LANES), LANES)
 
-    def multiply(c):
-        def against(e):
-            scores[part(c), part(e)] = lax.dot_general(
-                table[part(c), :width],
-                table[part(e), :width],
-                (((1,), (1,)), ((), ())),
-                preferred_element_type=jnp.float32,
-            )
-
-        repeat(chunks, against)
-
-    repeat(chunks, multiply)
+    for half in range(2):
+        repeat(depth, lambda place: arrival(place * 2 + 1 - x, half))
+        features = slice(half * width // 2, (half + 1) * width // 2)
+
+        def multiply(c):
+            def against(e):
+                product = lax.dot_general(
+                    table[part(c), features],
+                    table[part(e), features],
+                    (((1,), (1,)), ((), ())),
+                    preferred_element_type=jnp.float32,
+                )
+                if half == 1:
+                    product = product + scores[part(c), part(e)]
+                scores[part(c), part(e)] = product
+
+            repeat(chunks, against)
+
+        repeat(chunks, multiply)
 
     exchange = pltpu.make_async_remote_copy(
         src_ref=scores,
@@ -214,13 +244,13 @@
             is_document & jnp.logical_not(is_positive), logits[:, rows:], -jnp.inf
         )
         peak = jnp.max(jnp.maximum(query_logits, doc_logits), axis=2, keepdims=True)
-        mass = jnp.sum(
-            jnp.exp(query_logits - peak) + jnp.exp(doc_logits - peak), axis=2, keepdims=True
-        )
+        query_terms, doc_terms = jnp.exp(query_logits - peak), jnp.exp(doc_logits - peak)
+        mass = jnp.sum(query_terms + doc_terms, axis=2, keepdims=True)
         lse = peak + jnp.log(mass)
+        share = 1.0 / mass
         losses = lse - jnp.sum(jnp.where(is_positive, query_logits, 0.0), axis=2, keepdims=True)
         weights = jnp.concatenate(
-            [jnp.exp(query_logits - lse), jnp.exp(doc_logits - lse)], axis=1
+            [query_terms * share, doc_terms * share], axis=1
         )
         scores[part(c), :] = weights.reshape(LANES, total)
         landed[part(c), :LANES] = jnp.broadcast_to(
@@ -253,17 +283,23 @@
     at = lax.broadcasted_iota(jnp.int32, losses.shape, 0)
     loss_ref[...] = jnp.sum(jnp.where(across_place == at, losses, 0.0), axis=0, keepdims=True)
 
-    block_copy(me, twin, 0).wait_send()
-    repeat(depth - 1, lambda step: block_copy(me, twin, 1 + step).wait_send())
-    repeat(depth - 1, lambda step: block_copy(me, twin, depth + step).wait_send())
-
-
-def finish(width, left_ref, table_ref, loss_in, req_hbm, pas_hbm, loss_ref, req, pas, sem):
+    def drain(place):
+        for half in range(2):
+            sideward(place, half).wait_send()
+            pl.when(above & (place <= z))(lambda: upward(place, half).wait_send())
+            pl.when(below & (place >= z))(lambda: downward(place, half).wait_send())
+
+    repeat(depth, drain)
+
+
+def finish(width, left_ref, table_ref, loss_in, req_hbm, pas_hbm, loss_hbm, req, pas, loss, sem):
     rows = req.shape[0]
-    loss_ref[...] = loss_in[0, :rows]
+    loss[...] = loss_in[:, :rows]
+    loss_copy = pltpu.make_async_copy(loss, loss_hbm, sem.at[2 * PIECES])
+    loss_copy.start()
     total = left_ref.shape[1]
     step = width // PIECES
-    copies = []
+    copies = [loss_copy]
     for piece in range(PIECES):
         across = pl.ds(piece * step, step)
         out = jnp.zeros((4 * rows, step), jnp.float32)
@@ -311,8 +347,10 @@
             pltpu.VMEM((total, total), jnp.float32),
             pltpu.VMEM((LANES, LANES), jnp.float32),
             pltpu.SemaphoreType.DMA((4,)),
-            pltpu.SemaphoreType.DMA((n - 1,)),
-            pltpu.SemaphoreType.DMA((n,)),
+            pltpu.SemaphoreType.DMA((n // 2, 2)),
+            pltpu.SemaphoreType.DMA((n // 2, 2)),
+            pltpu.SemaphoreType.DMA((n // 2, 2)),
+            pltpu.SemaphoreType.DMA((n, 2)),
             pltpu.SemaphoreType.DMA((2,)),
         ],
         compiler_params=pltpu.CompilerParams(
@@ -324,22 +362,24 @@
     table, left, losses = (
         pltpu.with_memory_space_constraint(a, pltpu.VMEM) for a in (table, left, losses)
     )
-    return pl.pallas_call(
+    request, passage, losses = pl.pallas_call(
         functools.partial(finish, width),
         out_shape=(
             jax.ShapeDtypeStruct((rows, width), jnp.float32),
             jax.ShapeDtypeStruct((rows, width), jnp.float32),
-            jax.ShapeDtypeStruct((rows,), jnp.float32),
+            jax.ShapeDtypeStruct((1, rows), jnp.float32),
         ),
         in_specs=[vmem] * 3,
-        out_specs=(anywhere, anywhere, vmem),
+        out_specs=(anywhere,) * 3,
         scratch_shapes=[
             pltpu.VMEM((rows, width), jnp.float32),
             pltpu.VMEM((rows, width), jnp.float32),
-            pltpu.SemaphoreType.DMA((2 * PIECES,)),
+            pltpu.VMEM((1, rows), jnp.float32),
+            pltpu.SemaphoreType.DMA((2 * PIECES + 1,)),
         ],
         compiler_params=pltpu.CompilerParams(vmem_limit_bytes=6 * 1024 * 1024),
     )(left, table, losses)
+    return request, passage, losses.reshape(rows)
 
 
 def solution(mesh):

time: 19.8 us -> 20.4 us (1.030)
  Pallas kernels: 19 us -> 19.6 us
    pallas_call x1, Pallas kernels: 17.6 us -> 18.7 us  [on_device(): pl.pallas_call(functools.partial(kernel, n), out_shape=(pltpu.VMEM((total...]
    pallas_call x1, Pallas kernels: 1.38 us -> 0.88 us  [on_device(): pl.pallas_call(functools.partial(finish, width), out_shape=(jax.ShapeDtyp...]
where the time goes in v3:
time: 20.4 us; the launch traced here: 20.2 us
  Pallas kernels  19.6 us (96%)
  between operations  0.64 us (3%)
    pallas_call x1, Pallas kernels, on_device(): pl.pallas_call(functools.partial(kernel, n), out_shape=(pltpu.VMEM((total...  18.7 us
    pallas_call x1, Pallas kernels, on_device(): pl.pallas_call(functools.partial(finish, width), out_shape=(jax.ShapeDtyp...  0.88 us

profile of v3, /device:TPU:0, one launch (start us, length us, event | category | flops | bytes accessed | tf_op | source)
XLA Modules:
  0.0 20.2 jit_solution(8407188521981930145)
XLA Ops:
  0.6 18.7 %shard_map.67 = (bf16[128,2176]{1,0:T(8,128)(2,1)S(1)}, bf16[32,128]{1,0:T(8,128)(2,1)S(1)}, f32[1,128]{1,0:T(1,128)S(1)}) custom-call(f32[8,2048]{1,0:T(8,128)} %q_hbm.1, f32[8,2048]{1,0:T(8,128)} %d_hbm.1, s32[8]{0:T(128)} %pos_hbm.1, s32[8,7]{1,0:T(8,128)} %hid_hbm.1), custom_call_target="tpu_custom_call" | custom-call | tf_op jit(solution)/shard_map/pallas_call | solution.py:332
  19.3 0.9 %shard_map.68 = (f32[8,2048]{1,0:T(8,128)}, f32[8,2048]{1,0:T(8,128)}, f32[1,8]{1,0:T(1,128)}) custom-call(bf16[32,128]{1,0:T(8,128)(2,1)S(1)} %get-tuple-element.9.left_ref, bf16[128,2176]{1,0:T(8,128)(2,1)S(1)} %get-tuple-element.10.table_ref, f32[1,128]{1,0:T(1,128)S(1)} %get-tuple-element.11.loss_in), custom_call_target="tpu_custom_call" | custom-call | tf_op jit(solution)/shard_map/pallas_call | solution.py:365

commit v4 on v3

--- a/solution.py
+++ b/solution.py
@@ -55,7 +55,6 @@
     depth = n // 2
     z, x = me // 2, me % 2
     twin = z * 2 + (1 - x)
-    above, below = z + 1 < depth, z > 0
 
     def line(place):
         return place * 2 + x
@@ -76,8 +75,13 @@
 
     greet({"row": twin})
     greet({"col": 1 - core})
-    pl.when(above)(lambda: greet({"row": line(z + 1)}))
-    pl.when(below)(lambda: greet({"row": line(z - 1)}))
+
+    def greet_line(step):
+        high, low = z + step + 1, z - step - 1
+        pl.when(high < depth)(lambda: greet({"row": line(high)}))
+        pl.when(low >= 0)(lambda: greet({"row": line(low)}))
+
+    repeat(depth - 1, greet_line)
 
     for load in loads:
         load.wait()
@@ -118,7 +122,7 @@
         [to_documents(tally), jnp.zeros_like(tally)], axis=0
     ).astype(jnp.bfloat16)
 
-    pl.semaphore_wait(barrier, 2 + above.astype(jnp.int32) + below.astype(jnp.int32))
+    pl.semaphore_wait(barrier, depth + 1)
 
     halves = (pl.ds(0, width // 2), pl.ds(width // 2, width // 2 + total))
 
@@ -135,11 +139,16 @@
             device_id_type=MESH,
         )
 
-    def upward(place, half):
-        return block_copy(line(place), half, line(z + 1), up_sem.at[place, half])
-
-    def downward(place, half):
-        return block_copy(line(place), half, line(z - 1), down_sem.at[place, half])
+    def upward(far, half):
+        return block_copy(me, half, line(z + far), up_sem.at[far, half])
+
+    def downward(far, half):
+        return block_copy(me, half, line(z - far), down_sem.at[far, half])
+
+    def along(far, act):
+        for half in range(2):
+            pl.when(z + far < depth)(lambda: act(upward(far, half)))
+            pl.when(z - far >= 0)(lambda: act(downward(far, half)))
 
     def sideward(place, half):
         return block_copy(line(place), half, twin, side_sem.at[place, half])
@@ -147,9 +156,8 @@
     def arrival(source, half):
         block_copy(source, half, twin, side_sem.at[0, half]).wait_recv()
 
+    along(1, lambda copy: copy.start())
     for half in range(2):
-        pl.when(above)(lambda: upward(z, half).start())
-        pl.when(below)(lambda: downward(z, half).start())
         sideward(z, half).start()
 
     def relay(step):
@@ -159,14 +167,15 @@
             @pl.when(low >= 0)
             def _():
                 arrival(line(low), half)
-                pl.when(above)(lambda: upward(low, half).start())
                 sideward(low, half).start()
 
             @pl.when(high < depth)
             def _():
                 arrival(line(high), half)
-                pl.when(below)(lambda: downward(high, half).start())
                 sideward(high, half).start()
+
+            if half == 0:
+                along(step + 2, lambda copy: copy.start())
 
     repeat(depth - 1, relay)
 
@@ -286,10 +295,9 @@
     def drain(place):
         for half in range(2):
             sideward(place, half).wait_send()
-            pl.when(above & (place <= z))(lambda: upward(place, half).wait_send())
-            pl.when(below & (place >= z))(lambda: downward(place, half).wait_send())
 
     repeat(depth, drain)
+    repeat(depth - 1, lambda step: along(step + 1, lambda copy: copy.wait_send()))
 
 
 def finish(width, left_ref, table_ref, loss_in, req_hbm, pas_hbm, loss_hbm, req, pas, loss, sem):

time: 20.4 us -> 23.4 us (1.15)
  Pallas kernels: 19.6 us -> 22.6 us
    pallas_call x1, Pallas kernels: 18.7 us -> 21.7 us  [on_device(): pl.pallas_call(functools.partial(kernel, n), out_shape=(pltpu.VMEM((total...]
where the time goes in v4:
time: 23.4 us; the launch traced here: 23.2 us
  Pallas kernels  22.6 us (97%)
  between operations  0.64 us (3%)
    pallas_call x1, Pallas kernels, on_device(): pl.pallas_call(functools.partial(kernel, n), out_shape=(pltpu.VMEM((total...  21.7 us
    pallas_call x1, Pallas kernels, on_device(): pl.pallas_call(functools.partial(finish, width), out_shape=(jax.ShapeDtyp...  0.88 us

profile of v4, /device:TPU:0, one launch (start us, length us, event | category | flops | bytes accessed | tf_op | source)
XLA Modules:
  0.0 23.2 jit_solution(18010849772032614418)
XLA Ops:
  0.6 21.7 %shard_map.67 = (bf16[128,2176]{1,0:T(8,128)(2,1)S(1)}, bf16[32,128]{1,0:T(8,128)(2,1)S(1)}, f32[1,128]{1,0:T(1,128)S(1)}) custom-call(f32[8,2048]{1,0:T(8,128)} %q_hbm.1, f32[8,2048]{1,0:T(8,128)} %d_hbm.1, s32[8]{0:T(128)} %pos_hbm.1, s32[8,7]{1,0:T(8,128)} %hid_hbm.1), custom_call_target="tpu_custom_call" | custom-call | tf_op jit(solution)/shard_map/pallas_call | solution.py:340
  22.3 0.9 %shard_map.68 = (f32[8,2048]{1,0:T(8,128)}, f32[8,2048]{1,0:T(8,128)}, f32[1,8]{1,0:T(1,128)}) custom-call(bf16[32,128]{1,0:T(8,128)(2,1)S(1)} %get-tuple-element.9.left_ref, bf16[128,2176]{1,0:T(8,128)(2,1)S(1)} %get-tuple-element.10.table_ref, f32[1,128]{1,0:T(1,128)S(1)} %get-tuple-element.11.loss_in), custom_call_target="tpu_custom_call" | custom-call | tf_op jit(solution)/shard_map/pallas_call | solution.py:373

commit v5 on v4

--- a/solution.py
+++ b/solution.py
@@ -156,9 +156,9 @@
     def arrival(source, half):
         block_copy(source, half, twin, side_sem.at[0, half]).wait_recv()
 
-    along(1, lambda copy: copy.start())
     for half in range(2):
         sideward(z, half).start()
+    repeat(depth - 1, lambda step: along(step + 1, lambda copy: copy.start()))
 
     def relay(step):
         low, high = z - step - 1, z + step + 1
@@ -173,9 +173,6 @@
             def _():
                 arrival(line(high), half)
                 sideward(high, half).start()
-
-            if half == 0:
-                along(step + 2, lambda copy: copy.start())
 
     repeat(depth - 1, relay)
 

time: 23.4 us -> 19.8 us (0.85)
  Pallas kernels: 22.6 us -> 19 us
    pallas_call x1, Pallas kernels: 21.7 us -> 18.2 us  [on_device(): pl.pallas_call(functools.partial(kernel, n), out_shape=(pltpu.VMEM((total...]
where the time goes in v5:
time: 19.8 us; the launch traced here: 19.7 us
  Pallas kernels  19 us (96%)
  between operations  0.64 us (3%)
    pallas_call x1, Pallas kernels, on_device(): pl.pallas_call(functools.partial(kernel, n), out_shape=(pltpu.VMEM((total...  18.2 us
    pallas_call x1, Pallas kernels, on_device(): pl.pallas_call(functools.partial(finish, width), out_shape=(jax.ShapeDtyp...  0.88 us

profile of v5, /device:TPU:0, one launch (start us, length us, event | category | flops | bytes accessed | tf_op | source)
XLA Modules:
  0.0 19.7 jit_solution(12515796029571814258)
XLA Ops:
  0.6 18.2 %shard_map.67 = (bf16[128,2176]{1,0:T(8,128)(2,1)S(1)}, bf16[32,128]{1,0:T(8,128)(2,1)S(1)}, f32[1,128]{1,0:T(1,128)S(1)}) custom-call(f32[8,2048]{1,0:T(8,128)} %q_hbm.1, f32[8,2048]{1,0:T(8,128)} %d_hbm.1, s32[8]{0:T(128)} %pos_hbm.1, s32[8,7]{1,0:T(8,128)} %hid_hbm.1), custom_call_target="tpu_custom_call" | custom-call | tf_op jit(solution)/shard_map/pallas_call | solution.py:337
  18.8 0.9 %shard_map.68 = (f32[8,2048]{1,0:T(8,128)}, f32[8,2048]{1,0:T(8,128)}, f32[1,8]{1,0:T(1,128)}) custom-call(bf16[32,128]{1,0:T(8,128)(2,1)S(1)} %get-tuple-element.9.left_ref, bf16[128,2176]{1,0:T(8,128)(2,1)S(1)} %get-tuple-element.10.table_ref, f32[1,128]{1,0:T(1,128)S(1)} %get-tuple-element.11.loss_in), custom_call_target="tpu_custom_call" | custom-call | tf_op jit(solution)/shard_map/pallas_call | solution.py:370

commit v6 on v5

--- a/solution.py
+++ b/solution.py
@@ -12,6 +12,7 @@
 MESH = pl.DeviceIdType.MESH
 LANES = 128
 PIECES = 2
+SHARES = 1
 
 
 def repeat(count, body):
@@ -124,7 +125,7 @@
 
     pl.semaphore_wait(barrier, depth + 1)
 
-    halves = (pl.ds(0, width // 2), pl.ds(width // 2, width // 2 + total))
+    halves = (pl.ds(0, width + total),)
 
     def block_copy(source, half, target, sem):
         block = table.at[
@@ -146,7 +147,7 @@
         return block_copy(me, half, line(z - far), down_sem.at[far, half])
 
     def along(far, act):
-        for half in range(2):
+        for half in range(SHARES):
             pl.when(z + far < depth)(lambda: act(upward(far, half)))
             pl.when(z - far >= 0)(lambda: act(downward(far, half)))
 
@@ -156,13 +157,13 @@
     def arrival(source, half):
         block_copy(source, half, twin, side_sem.at[0, half]).wait_recv()
 
-    for half in range(2):
+    for half in range(SHARES):
         sideward(z, half).start()
     repeat(depth - 1, lambda step: along(step + 1, lambda copy: copy.start()))
 
     def relay(step):
         low, high = z - step - 1, z + step + 1
-        for half in range(2):
+        for half in range(SHARES):
 
             @pl.when(low >= 0)
             def _():
@@ -180,9 +181,9 @@
         start = c * LANES
         return pl.ds(start if isinstance(c, int) else pl.multiple_of(start, LANES), LANES)
 
-    for half in range(2):
+    for half in range(SHARES):
         repeat(depth, lambda place: arrival(place * 2 + 1 - x, half))
-        features = slice(half * width // 2, (half + 1) * width // 2)
+        features = slice(half * width // SHARES, (half + 1) * width // SHARES)
 
         def multiply(c):
             def against(e):
@@ -192,7 +193,7 @@
                     (((1,), (1,)), ((), ())),
                     preferred_element_type=jnp.float32,
                 )
-                if half == 1:
+                if half > 0:
                     product = product + scores[part(c), part(e)]
                 scores[part(c), part(e)] = product
 
@@ -290,7 +291,7 @@
     loss_ref[...] = jnp.sum(jnp.where(across_place == at, losses, 0.0), axis=0, keepdims=True)
 
     def drain(place):
-        for half in range(2):
+        for half in range(SHARES):
             sideward(place, half).wait_send()
 
     repeat(depth, drain)
@@ -352,10 +353,10 @@
             pltpu.VMEM((total, total), jnp.float32),
             pltpu.VMEM((LANES, LANES), jnp.float32),
             pltpu.SemaphoreType.DMA((4,)),
-            pltpu.SemaphoreType.DMA((n // 2, 2)),
-            pltpu.SemaphoreType.DMA((n // 2, 2)),
-            pltpu.SemaphoreType.DMA((n // 2, 2)),
-            pltpu.SemaphoreType.DMA((n, 2)),
+            pltpu.SemaphoreType.DMA((n // 2, SHARES)),
+            pltpu.SemaphoreType.DMA((n // 2, SHARES)),
+            pltpu.SemaphoreType.DMA((n // 2, SHARES)),
+            pltpu.SemaphoreType.DMA((n, SHARES)),
             pltpu.SemaphoreType.DMA((2,)),
         ],
         compiler_params=pltpu.CompilerParams(

time: 19.8 us -> 20 us (1.010)
  no operation moved by 1% of the time
where the time goes in v6:
time: 20 us; the launch traced here: 19.9 us
  Pallas kernels  19.2 us (96%)
  between operations  0.64 us (3%)
    pallas_call x1, Pallas kernels, on_device(): pl.pallas_call(functools.partial(kernel, n), out_shape=(pltpu.VMEM((total...  18.3 us
    pallas_call x1, Pallas kernels, on_device(): pl.pallas_call(functools.partial(finish, width), out_shape=(jax.ShapeDtyp...  0.88 us

profile of v6, /device:TPU:0, one launch (start us, length us, event | category | flops | bytes accessed | tf_op | source)
XLA Modules:
  0.0 19.9 jit_solution(5010957926219208483)
XLA Ops:
  0.6 18.3 %shard_map.67 = (bf16[128,2176]{1,0:T(8,128)(2,1)S(1)}, bf16[32,128]{1,0:T(8,128)(2,1)S(1)}, f32[1,128]{1,0:T(1,128)S(1)}) custom-call(f32[8,2048]{1,0:T(8,128)} %q_hbm.1, f32[8,2048]{1,0:T(8,128)} %d_hbm.1, s32[8]{0:T(128)} %pos_hbm.1, s32[8,7]{1,0:T(8,128)} %hid_hbm.1), custom_call_target="tpu_custom_call" | custom-call | tf_op jit(solution)/shard_map/pallas_call | solution.py:338
  19.0 0.9 %shard_map.68 = (f32[8,2048]{1,0:T(8,128)}, f32[8,2048]{1,0:T(8,128)}, f32[1,8]{1,0:T(1,128)}) custom-call(bf16[32,128]{1,0:T(8,128)(2,1)S(1)} %get-tuple-element.9.left_ref, bf16[128,2176]{1,0:T(8,128)(2,1)S(1)} %get-tuple-element.10.table_ref, f32[1,128]{1,0:T(1,128)S(1)} %get-tuple-element.11.loss_in), custom_call_target="tpu_custom_call" | custom-call | tf_op jit(solution)/shard_map/pallas_call | solution.py:371

commit v7 on v2

--- a/solution.py
+++ b/solution.py
@@ -50,15 +50,12 @@
     per_chunk = LANES // pair_rows
     me = lax.axis_index("row")
     core = lax.axis_index("col")
-    depth = n // 2
-    z, x = me // 2, me % 2
-    twin = z * 2 + (1 - x)
-
-    def line_peer(step):
-        return lax.rem(z + step + 1, depth) * 2 + x
-
-    def line_source(step):
-        return lax.rem(z + depth - step - 1, depth) * 2 + x
+
+    def peer(step):
+        return lax.rem(me + step + 1, n)
+
+    def source(step):
+        return lax.rem(me + n - step - 1, n)
 
     loads = [
         pltpu.make_async_copy(src, dst, in_sem.at[i])
@@ -71,14 +68,11 @@
 
     barrier = pltpu.get_barrier_semaphore()
 
-    def greet(step):
-        pl.semaphore_signal(
-            barrier, inc=1, device_id={"row": line_peer(step)}, device_id_type=MESH
-        )
-
-    repeat(depth - 1, greet)
-    pl.semaphore_signal(barrier, inc=1, device_id={"row": twin}, device_id_type=MESH)
-    pl.semaphore_signal(barrier, inc=1, device_id={"col": 1 - core}, device_id_type=MESH)
+    def greet(device):
+        pl.semaphore_signal(barrier, inc=1, device_id=device, device_id_type=MESH)
+
+    greet({"col": 1 - core})
+    repeat(n - 1, lambda step: greet({"row": peer(step)}))
 
     for load in loads:
         load.wait()
@@ -119,33 +113,21 @@
         [to_documents(tally), jnp.zeros_like(tally)], axis=0
     ).astype(jnp.bfloat16)
 
-    pl.semaphore_wait(barrier, depth + 1)
-
-    def block_copy(source, target, slot):
-        block = table.at[pl.ds(pl.multiple_of(source * pair_rows, pair_rows), pair_rows)]
+    pl.semaphore_wait(barrier, n)
+
+    def block_copy(owner, target, slot):
+        block = table.at[pl.ds(pl.multiple_of(owner * pair_rows, pair_rows), pair_rows)]
         return pltpu.make_async_remote_copy(
             src_ref=block,
             dst_ref=block,
             send_sem=send_sem.at[slot],
-            recv_sem=recv_sem.at[source],
+            recv_sem=recv_sem.at[owner],
             device_id={"row": target},
             device_id_type=MESH,
         )
 
-    block_copy(me, twin, 0).start()
-    repeat(depth - 1, lambda step: block_copy(me, line_peer(step), 1 + step).start())
-
-    def forward(step):
-        source = line_source(step)
-        block_copy(source, twin, depth + step).wait_recv()
-        block_copy(source, twin, depth + step).start()
-
-    repeat(depth - 1, forward)
-    block_copy(twin, twin, 0).wait_recv()
-    repeat(
-        depth - 1,
-        lambda step: block_copy(line_source(step) + 1 - 2 * x, twin, 0).wait_recv(),
-    )
+    repeat(n - 1, lambda step: block_copy(me, peer(step), step).start())
+    repeat(n - 1, lambda step: block_copy(source(step), peer(0), 0).wait_recv())
 
     def part(c):
         start = c * LANES
@@ -214,13 +196,13 @@
             is_document & jnp.logical_not(is_positive), logits[:, rows:], -jnp.inf
         )
         peak = jnp.max(jnp.maximum(query_logits, doc_logits), axis=2, keepdims=True)
-        mass = jnp.sum(
-            jnp.exp(query_logits - peak) + jnp.exp(doc_logits - peak), axis=2, keepdims=True
-        )
+        query_terms, doc_terms = jnp.exp(query_logits - peak), jnp.exp(doc_logits - peak)
+        mass = jnp.sum(query_terms + doc_terms, axis=2, keepdims=True)
         lse = peak + jnp.log(mass)
+        share = 1.0 / mass
         losses = lse - jnp.sum(jnp.where(is_positive, query_logits, 0.0), axis=2, keepdims=True)
         weights = jnp.concatenate(
-            [jnp.exp(query_logits - lse), jnp.exp(doc_logits - lse)], axis=1
+            [query_terms * share, doc_terms * share], axis=1
         )
         scores[part(c), :] = weights.reshape(LANES, total)
         landed[part(c), :LANES] = jnp.broadcast_to(
@@ -253,17 +235,17 @@
     at = lax.broadcasted_iota(jnp.int32, losses.shape, 0)
     loss_ref[...] = jnp.sum(jnp.where(across_place == at, losses, 0.0), axis=0, keepdims=True)
 
-    block_copy(me, twin, 0).wait_send()
-    repeat(depth - 1, lambda step: block_copy(me, twin, 1 + step).wait_send())
-    repeat(depth - 1, lambda step: block_copy(me, twin, depth + step).wait_send())
-
-
-def finish(width, left_ref, table_ref, loss_in, req_hbm, pas_hbm, loss_ref, req, pas, sem):
+    repeat(n - 1, lambda step: block_copy(me, peer(step), step).wait_send())
+
+
+def finish(width, left_ref, table_ref, loss_in, req_hbm, pas_hbm, loss_hbm, req, pas, loss, sem):
     rows = req.shape[0]
-    loss_ref[...] = loss_in[0, :rows]
+    loss[...] = loss_in[:, :rows]
+    loss_copy = pltpu.make_async_copy(loss, loss_hbm, sem.at[2 * PIECES])
+    loss_copy.start()
     total = left_ref.shape[1]
     step = width // PIECES
-    copies = []
+    copies = [loss_copy]
     for piece in range(PIECES):
         across = pl.ds(piece * step, step)
         out = jnp.zeros((4 * rows, step), jnp.float32)
@@ -324,22 +306,24 @@
     table, left, losses = (
         pltpu.with_memory_space_constraint(a, pltpu.VMEM) for a in (table, left, losses)
     )
-    return pl.pallas_call(
+    request, passage, losses = pl.pallas_call(
         functools.partial(finish, width),
         out_shape=(
             jax.ShapeDtypeStruct((rows, width), jnp.float32),
             jax.ShapeDtypeStruct((rows, width), jnp.float32),
-            jax.ShapeDtypeStruct((rows,), jnp.float32),
+            jax.ShapeDtypeStruct((1, rows), jnp.float32),
         ),
         in_specs=[vmem] * 3,
-        out_specs=(anywhere, anywhere, vmem),
+        out_specs=(anywhere,) * 3,
         scratch_shapes=[
             pltpu.VMEM((rows, width), jnp.float32),
             pltpu.VMEM((rows, width), jnp.float32),
-            pltpu.SemaphoreType.DMA((2 * PIECES,)),
+            pltpu.VMEM((1, rows), jnp.float32),
+            pltpu.SemaphoreType.DMA((2 * PIECES + 1,)),
         ],
         compiler_params=pltpu.CompilerParams(vmem_limit_bytes=6 * 1024 * 1024),
     )(left, table, losses)
+    return request, passage, losses.reshape(rows)
 
 
 def solution(mesh):

time: 19.8 us -> 20.5 us (1.035)
  the two profiles are of different devices: /device:TPU:0 before, /device:TPU:11 now
where the time goes in v7:
time: 20.5 us; the launch traced here: 20.3 us
  Pallas kernels  19.7 us (96%)
  between operations  0.64 us (3%)
    pallas_call x1, Pallas kernels, on_device(): pl.pallas_call(functools.partial(kernel, n), out_shape=(pltpu.VMEM((total...  18.8 us
    pallas_call x1, Pallas kernels, on_device(): pl.pallas_call(functools.partial(finish, width), out_shape=(jax.ShapeDtyp...  0.88 us

profile of v7, /device:TPU:11, one launch (start us, length us, event | category | flops | bytes accessed | tf_op | source)
XLA Modules:
  0.0 20.3 jit_solution(462023508992394727)
XLA Ops:
  0.6 18.8 %shard_map.67 = (bf16[128,2176]{1,0:T(8,128)(2,1)S(1)}, bf16[32,128]{1,0:T(8,128)(2,1)S(1)}, f32[1,128]{1,0:T(1,128)S(1)}) custom-call(f32[8,2048]{1,0:T(8,128)} %q_hbm.1, f32[8,2048]{1,0:T(8,128)} %d_hbm.1, s32[8]{0:T(128)} %pos_hbm.1, s32[8,7]{1,0:T(8,128)} %hid_hbm.1), custom_call_target="tpu_custom_call" | custom-call | tf_op jit(solution)/shard_map/pallas_call | solution.py:278
  19.4 0.9 %shard_map.68 = (f32[8,2048]{1,0:T(8,128)}, f32[8,2048]{1,0:T(8,128)}, f32[1,8]{1,0:T(1,128)}) custom-call(bf16[32,128]{1,0:T(8,128)(2,1)S(1)} %get-tuple-element.9.left_ref, bf16[128,2176]{1,0:T(8,128)(2,1)S(1)} %get-tuple-element.10.table_ref, f32[1,128]{1,0:T(1,128)S(1)} %get-tuple-element.11.loss_in), custom_call_target="tpu_custom_call" | custom-call | tf_op jit(solution)/shard_map/pallas_call | solution.py:309

commit v8 on v2

--- a/solution.py
+++ b/solution.py
@@ -214,13 +214,13 @@
             is_document & jnp.logical_not(is_positive), logits[:, rows:], -jnp.inf
         )
         peak = jnp.max(jnp.maximum(query_logits, doc_logits), axis=2, keepdims=True)
-        mass = jnp.sum(
-            jnp.exp(query_logits - peak) + jnp.exp(doc_logits - peak), axis=2, keepdims=True
-        )
+        query_terms, doc_terms = jnp.exp(query_logits - peak), jnp.exp(doc_logits - peak)
+        mass = jnp.sum(query_terms + doc_terms, axis=2, keepdims=True)
         lse = peak + jnp.log(mass)
+        share = 1.0 / mass
         losses = lse - jnp.sum(jnp.where(is_positive, query_logits, 0.0), axis=2, keepdims=True)
         weights = jnp.concatenate(
-            [jnp.exp(query_logits - lse), jnp.exp(doc_logits - lse)], axis=1
+            [query_terms * share, doc_terms * share], axis=1
         )
         scores[part(c), :] = weights.reshape(LANES, total)
         landed[part(c), :LANES] = jnp.broadcast_to(
@@ -258,12 +258,14 @@
     repeat(depth - 1, lambda step: block_copy(me, twin, depth + step).wait_send())
 
 
-def finish(width, left_ref, table_ref, loss_in, req_hbm, pas_hbm, loss_ref, req, pas, sem):
+def finish(width, left_ref, table_ref, loss_in, req_hbm, pas_hbm, loss_hbm, req, pas, loss, sem):
     rows = req.shape[0]
-    loss_ref[...] = loss_in[0, :rows]
+    loss[...] = loss_in[:, :rows]
+    loss_copy = pltpu.make_async_copy(loss, loss_hbm, sem.at[2 * PIECES])
+    loss_copy.start()
     total = left_ref.shape[1]
     step = width // PIECES
-    copies = []
+    copies = [loss_copy]
     for piece in range(PIECES):
         across = pl.ds(piece * step, step)
         out = jnp.zeros((4 * rows, step), jnp.float32)
@@ -324,22 +326,24 @@
     table, left, losses = (
         pltpu.with_memory_space_constraint(a, pltpu.VMEM) for a in (table, left, losses)
     )
-    return pl.pallas_call(
+    request, passage, losses = pl.pallas_call(
         functools.partial(finish, width),
         out_shape=(
             jax.ShapeDtypeStruct((rows, width), jnp.float32),
             jax.ShapeDtypeStruct((rows, width), jnp.float32),
-            jax.ShapeDtypeStruct((rows,), jnp.float32),
+            jax.ShapeDtypeStruct((1, rows), jnp.float32),
         ),
         in_specs=[vmem] * 3,
-        out_specs=(anywhere, anywhere, vmem),
+        out_specs=(anywhere,) * 3,
         scratch_shapes=[
             pltpu.VMEM((rows, width), jnp.float32),
             pltpu.VMEM((rows, width), jnp.float32),
-            pltpu.SemaphoreType.DMA((2 * PIECES,)),
+            pltpu.VMEM((1, rows), jnp.float32),
+            pltpu.SemaphoreType.DMA((2 * PIECES + 1,)),
         ],
         compiler_params=pltpu.CompilerParams(vmem_limit_bytes=6 * 1024 * 1024),
     )(left, table, losses)
+    return request, passage, losses.reshape(rows)
 
 
 def solution(mesh):

time: 19.8 us -> 19.3 us (0.975)
  Pallas kernels: 19 us -> 18.5 us
    pallas_call x1, Pallas kernels: 1.38 us -> 0.88 us  [on_device(): pl.pallas_call(functools.partial(finish, width), out_shape=(jax.ShapeDtyp...]
where the time goes in v8:
time: 19.3 us; the launch traced here: 19.1 us
  Pallas kernels  18.5 us (96%)
  between operations  0.64 us (3%)
    pallas_call x1, Pallas kernels, on_device(): pl.pallas_call(functools.partial(kernel, n), out_shape=(pltpu.VMEM((total...  17.6 us
    pallas_call x1, Pallas kernels, on_device(): pl.pallas_call(functools.partial(finish, width), out_shape=(jax.ShapeDtyp...  0.88 us

profile of v8, /device:TPU:0, one launch (start us, length us, event | category | flops | bytes accessed | tf_op | source)
XLA Modules:
  0.0 19.1 jit_solution(2656350277187689682)
XLA Ops:
  0.6 17.6 %shard_map.67 = (bf16[128,2176]{1,0:T(8,128)(2,1)S(1)}, bf16[32,128]{1,0:T(8,128)(2,1)S(1)}, f32[1,128]{1,0:T(1,128)S(1)}) custom-call(f32[8,2048]{1,0:T(8,128)} %q_hbm.1, f32[8,2048]{1,0:T(8,128)} %d_hbm.1, s32[8]{0:T(128)} %pos_hbm.1, s32[8,7]{1,0:T(8,128)} %hid_hbm.1), custom_call_target="tpu_custom_call" | custom-call | tf_op jit(solution)/shard_map/pallas_call | solution.py:298
  18.2 0.9 %shard_map.68 = (f32[8,2048]{1,0:T(8,128)}, f32[8,2048]{1,0:T(8,128)}, f32[1,8]{1,0:T(1,128)}) custom-call(bf16[32,128]{1,0:T(8,128)(2,1)S(1)} %get-tuple-element.9.left_ref, bf16[128,2176]{1,0:T(8,128)(2,1)S(1)} %get-tuple-element.10.table_ref, f32[1,128]{1,0:T(1,128)S(1)} %get-tuple-element.11.loss_in), custom_call_target="tpu_custom_call" | custom-call | tf_op jit(solution)/shard_map/pallas_call | solution.py:329
